TPU v7x, 32 devices: a whole 2x2x4 slice. The times are simulated.
32 devices in a mesh: bead: 4 (over y, x), wave: 4 (over z), grp: 2 (over core).
Axes of the slice: x: 2, y: 2, z: 4, core: 2. Of those that a mesh axis runs over, the one named last changes fastest.
Arguments:
- features: float32 [4096, 512], P(('bead', 'wave', 'grp')), may hold values from -6 to 6
- positions: float32 [3, 4096], P(None, ('bead', 'wave', 'grp')), may hold values from 0 to 1
- wavevectors: int32 [3, 4096], P(None, ('wave', 'grp')), may hold values from -6 to 6
- neighbour_slots: int32 [32, 4096], P(None, ('bead', 'wave', 'grp')), may hold values from 0 to 383
- neighbour_count: int32 [4096], P(('bead', 'wave', 'grp')), may hold values from 8 to 32
- pair_distance: float32 [32, 4096], P(None, ('bead', 'wave', 'grp')), may hold values from 0.3 to 2.4
- w_self: float32 [512, 512], replicated, may hold values from -0.25 to 0.25
- w_neighbour: float32 [512, 512], replicated, may hold values from -0.25 to 0.25
- w_edge: float32 [16, 512], replicated, may hold values from -1.5 to 1.5
- w_message: float32 [512, 512], replicated, may hold values from -0.25 to 0.25
- spec_filter: float32 [4096, 512], P(('wave', 'grp')), may hold values from -4 to 4
- norm_gain: float32 [512], replicated, may hold values from 0.5 to 1.5
- w_up: float32 [512, 512], replicated, may hold values from -0.25 to 0.25
- w_down: float32 [512, 512], replicated, may hold values from -0.25 to 0.25
Outputs:
- updated: float32 [4096, 512], P(('bead', 'wave', 'grp'))
All inputs are finite; a program needn't handle non-finite values.
Results may differ from a plain program's by a relative error of at most 0.0003.
Values sent between devices are 32-bit elements; how exact they have to be, the bound alone decides.
A program may use at most 128 MiB of HBM per device.

v0:
```python
import functools

import jax
import jax.numpy as jnp
from jax import lax
from jax.experimental import pallas as pl
from jax.experimental.pallas import tpu as pltpu
from jax.sharding import PartitionSpec as P

MESH = pl.DeviceIdType.MESH
F32, BF16 = jnp.float32, jnp.bfloat16
BLOCK = 128
TOP = 6
HALF = TOP + 1
TAB = 8
REACH = 2.5
EPS = 1e-05
TWO_PI = 6.283185307179586
GROUP = 4
SLOTS = 4


def split(x):
    hi = x.astype(BF16)
    return hi, (x - hi.astype(F32)).astype(BF16)


def dot(a, b, ca=1, cb=0):
    return lax.dot_general(a, b, (((ca,), (cb,)), ((), ())), preferred_element_type=F32)


def mm3(a, b, ca=1, cb=0):
    return dot(a[0], b[0], ca, cb) + (dot(a[0], b[1], ca, cb) + dot(a[1], b[0], ca, cb))


def body(
    sizes,
    feat_ref, pos_ref, spack_ref, slot_ref, count_ref, dist_ref,
    wself_ref, wneigh_ref, wedge_ref, wmsg_ref, gain_ref, wup_ref, wdown_ref,
    out_ref,
    pack, fall, spall, halo, xyh, xyl, ztab, ytab, ah, al, tacc, lng, back, lt,
    wt, selft, acc, gacc,
    fs, fr, ss, sr, hs, hr, bs, br,
):
    nb, nw, ng = sizes
    n, nj = nb * nw * ng, nw * ng
    rows, width = feat_ref.shape
    fpd = width // n
    fp = max(fpd, 16)
    cf = TAB * fp
    ch = GROUP * BLOCK
    nq = n // GROUP
    kloc = spack_ref.shape[2]
    ib, iw, ig = lax.axis_index("bead"), lax.axis_index("wave"), lax.axis_index("grp")
    mine = iw * ng + ig
    me = ib * nj + mine

    def coords(p):
        return (lax.div(p, nj), lax.rem(lax.div(p, ng), nw), lax.rem(p, ng))

    barrier = pltpu.get_barrier_semaphore()

    def greet(t, _):
        pl.semaphore_signal(barrier, inc=1, device_id=coords(lax.rem(me + t, n)), device_id_type=MESH)
        return 0

    lax.fori_loop(1, n, greet, 0)

    ft = feat_ref[...].T
    angle = TWO_PI * pos_ref[...]
    trig = jnp.concatenate([jnp.cos(angle), jnp.sin(angle)], axis=0)
    for p in range(n):
        pack[p, 0:fpd, :] = ft[p * fpd : (p + 1) * fpd]
        pack[p, fpd : fpd + 6, :] = trig
    pl.semaphore_wait(barrier, n - 1)

    def feat_copy(p, slot):
        return pltpu.make_async_remote_copy(
            src_ref=pack.at[p], dst_ref=fall.at[slot], send_sem=fs.at[p], recv_sem=fr.at[slot],
            device_id=coords(p), device_id_type=MESH)

    def spec_copy(j, slot):
        return pltpu.make_async_remote_copy(
            src_ref=spack_ref.at[j], dst_ref=spall.at[slot], send_sem=ss.at[j], recv_sem=sr.at[slot],
            device_id=coords(ib * nj + j), device_id_type=MESH)

    def halo_copy(side):
        p = me + 1 if side == 0 else me - 1
        return pltpu.make_async_remote_copy(
            src_ref=feat_ref, dst_ref=halo.at[side], send_sem=hs.at[side], recv_sem=hr.at[side],
            device_id=coords(p), device_id_type=MESH)

    def back_copy(p, slot):
        return pltpu.make_async_remote_copy(
            src_ref=lng.at[p], dst_ref=back.at[slot], send_sem=bs.at[p], recv_sem=br.at[slot],
            device_id=coords(p), device_id_type=MESH)

    @pl.when(me + 1 < n)
    def _():
        halo_copy(0).start()

    @pl.when(me > 0)
    def _():
        halo_copy(1).start()

    def send_feat(t, _):
        feat_copy(lax.rem(me + t, n), me).start()
        return 0

    lax.fori_loop(1, n, send_feat, 0)

    def send_spec(t, _):
        spec_copy(lax.rem(mine + t, nj), mine).start()
        return 0

    lax.fori_loop(1, nj, send_spec, 0)
    fall[pl.ds(me, 1)] = pack[pl.ds(me, 1)]
    spall[pl.ds(mine, 1)] = spack_ref[pl.ds(mine, 1)]

    @pl.when(me == 0)
    def _():
        halo[0] = jnp.zeros((rows, width), F32)

    @pl.when(me == n - 1)
    def _():
        halo[1] = jnp.zeros((rows, width), F32)

    own = split(feat_ref[...])
    selft[...] = 0.5 * mm3(own, split(wself_ref[...])).T
    wn = split(wneigh_ref[...])
    span = 3 * BLOCK

    def put_window(at, part):
        hi, lo = split(0.5 * mm3(part, wn).T)
        wt[:, at * BLOCK : (at + 1) * BLOCK] = hi
        wt[:, span + at * BLOCK : span + (at + 1) * BLOCK] = lo

    put_window(1, own)
    radial = wedge_ref.shape[0]
    eh, el = split(0.5 * wedge_ref[...].T)
    wt[:, 2 * span : 2 * span + BLOCK] = jnp.concatenate(
        [eh, eh, el, jnp.zeros((width, BLOCK - 3 * radial), BF16)], axis=1)

    @pl.when(me > 0)
    def _():
        halo_copy(0).wait_recv()

    @pl.when(me + 1 < n)
    def _():
        halo_copy(1).wait_recv()

    put_window(0, split(halo[0]))
    put_window(2, split(halo[1]))

    acc[...] = jnp.zeros((width, rows), F32)
    spacing = REACH / (radial - 1)
    centers = lax.broadcasted_iota(jnp.int32, (radial, rows), 0).astype(F32) * spacing
    row_id = lax.broadcasted_iota(jnp.int32, (span, rows), 0)
    slots = slot_ref.shape[0]
    count = count_ref[...]

    def short_step(t, _):
        parts = []
        for u in range(SLOTS):
            s = t * SLOTS + u
            one = jnp.where(row_id == slot_ref[pl.ds(s, 1), :], 1.0, 0.0).astype(BF16)
            bh, bl = split(jnp.exp(-jnp.square((dist_ref[pl.ds(s, 1), :] - centers) / spacing)))
            parts.append(jnp.concatenate(
                [one, one, bh, bl, bh, jnp.zeros((BLOCK - 3 * radial, rows), BF16)], axis=0))
        pre = dot(wt[...], jnp.concatenate(parts, axis=1))
        total = acc[...]
        for u in range(SLOTS):
            h = pre[:, u * rows : (u + 1) * rows] + selft[...]
            live = count > t * SLOTS + u
            total = total + jnp.where(live, h + h * jnp.tanh(h), 0.0)
        acc[...] = total
        return 0

    lax.fori_loop(0, slots // SLOTS, short_step, 0)
    short = mm3(split((acc[...] * (1.0 / slots)).T), split(wmsg_ref[...]))
    out_ref[...] = feat_ref[...] + short

    def wait_spec(t, _):
        j = lax.rem(mine + t, nj)
        spec_copy(j, j).wait_recv()
        return 0

    lax.fori_loop(1, nj, wait_spec, 0)
    nvec = 4 * HALF * TAB
    gacc[...] = jnp.zeros(gacc.shape, F32)

    def spec_step(j, _):
        sp = spall[j, 0:fpd, :]
        if fp > fpd:
            sp = jnp.concatenate([sp, jnp.zeros((fp - fpd, kloc), F32)], axis=0)
        kx, ky, kz = (spall[j, fpd + i : fpd + i + 1, :] for i in range(3))
        flip = jnp.where(kx < 0, -1.0, 1.0)
        ky, kz = ky * flip, kz * flip
        kind = jnp.where(ky < 0, 2.0, 0.0) + jnp.where(kz < 0, 1.0, 0.0)
        at = kind * (HALF * TAB) + jnp.abs(kx) * TAB + jnp.abs(ky)
        vec_id = lax.broadcasted_iota(jnp.int32, (nvec, kloc), 0).astype(F32)
        pick = jnp.where(vec_id == at, 1.0, 0.0).astype(BF16)
        c = jnp.abs(kz)
        vals = jnp.concatenate([jnp.where(c == i, sp, 0.0) for i in range(TAB)], axis=0)
        hits = jnp.concatenate(
            [jnp.broadcast_to(jnp.where(c == i, 1.0, 0.0), (fp, kloc)) for i in range(TAB)], axis=0)
        vh, vl = split(vals)
        gacc[...] += dot(pick, jnp.concatenate([vh, vl, hits.astype(BF16)], axis=0), 1, 1)
        return 0

    lax.fori_loop(0, nj, spec_step, 0)

    tacc[...] = jnp.zeros(tacc.shape, F32)

    def fwd_step(t, _):
        q = lax.rem(lax.div(me, GROUP) + t, nq)
        for i in range(GROUP):
            p = q * GROUP + i

            @pl.when(p != me)
            def _():
                feat_copy(p, p).wait_recv()

        blocks = [fall[q * GROUP + i] for i in range(GROUP)]
        f = jnp.concatenate([b[0:fpd] for b in blocks], axis=1)
        if fp > fpd:
            f = jnp.concatenate([f, jnp.zeros((fp - fpd, ch), F32)], axis=0)
        c1 = jnp.concatenate([b[fpd : fpd + 3] for b in blocks], axis=1)
        s1 = jnp.concatenate([b[fpd + 3 : fpd + 6] for b in blocks], axis=1)
        cs, sn = [jnp.ones_like(c1), c1], [jnp.zeros_like(c1), s1]
        for a in range(2, HALF):
            cs.append(cs[-1] * c1 - sn[-1] * s1)
            sn.append(sn[-1] * c1 + cs[-2] * s1)
        zero = jnp.zeros((1, ch), F32)
        for a in range(HALF):
            ytab[a : a + 1, :] = cs[a][1:2]
            ytab[TAB + a : TAB + a + 1, :] = sn[a][1:2]
            ztab[q, a : a + 1, :] = cs[a][2:3]
            ztab[q, TAB + a : TAB + a + 1, :] = sn[a][2:3]
        for a in (HALF, TAB + HALF):
            ytab[a : a + 1, :] = zero
            ztab[q, a : a + 1, :] = zero
        yt = ytab[...]
        for a in range(2 * HALF):
            x = cs[a][0:1] if a < HALF else sn[a - HALF][0:1]
            hi, lo = split(x * yt)
            xyh[q, a * 2 * TAB : (a + 1) * 2 * TAB, :] = hi
            xyl[q, a * 2 * TAB : (a + 1) * 2 * TAB, :] = lo
        for c in range(2 * TAB):
            hi, lo = split(ztab[q, c : c + 1, :] * f)
            ah[c * fp : (c + 1) * fp, :] = hi
            al[c * fp : (c + 1) * fp, :] = lo
        tacc[...] += mm3((xyh[q], xyl[q]), (ah[...], al[...]), 1, 1)
        return 0

    lax.fori_loop(0, nq, fwd_step, 0)

    nt = HALF * TAB
    t3 = tacc[...].reshape(2 * HALF, 2 * TAB, 2 * cf)

    def get(x, y, z):
        return t3[x * HALF : (x + 1) * HALF, y * TAB : (y + 1) * TAB, z * cf : (z + 1) * cf].reshape(nt, cf)

    ccc, ccs, csc, css = get(0, 0, 0), get(0, 0, 1), get(0, 1, 0), get(0, 1, 1)
    scc, scs, ssc, sss = get(1, 0, 0), get(1, 0, 1), get(1, 1, 0), get(1, 1, 1)
    pairs, power = [], jnp.zeros((1, cf), F32)
    for v, (b, c) in enumerate(((1, 1), (1, -1), (-1, 1), (-1, -1))):
        cosf = ccc - b * ssc - c * scs - (b * c) * css
        sinf = scc + b * csc + c * ccs - (b * c) * sss
        hits = gacc[v * nt : (v + 1) * nt, 2 * cf : 3 * cf]
        power = power + jnp.sum(hits * (cosf * cosf + sinf * sinf), axis=0, keepdims=True)
        pairs.append((b, c, cosf, sinf))
    for i in range(3):
        power = power + pltpu.roll(power, fp << i, 1)
    kvec = nj * kloc
    scale = lax.rsqrt(power / (2 * kvec) + EPS) * (1.0 / kvec**0.5)
    grid = [jnp.zeros((nt, cf), F32)] * 8
    for v, (b, c, cosf, sinf) in enumerate(pairs):
        g = (gacc[v * nt : (v + 1) * nt, 0:cf] + gacc[v * nt : (v + 1) * nt, cf : 2 * cf]) * scale
        fc, fsn = g * cosf, g * sinf
        signs = (1, c, b, -b * c, 1, -c, -b, -b * c)
        picks = (fc, fsn, fsn, fc, fsn, fc, fc, fsn)
        grid = [old + s * x for old, s, x in zip(grid, signs, picks)]
    g3 = [x.reshape(HALF, TAB, cf) for x in grid]
    plane = [jnp.concatenate([g3[2 * i], g3[2 * i + 1]], axis=2) for i in range(4)]
    half = [jnp.concatenate([plane[2 * i], plane[2 * i + 1]], axis=1) for i in range(2)]
    tt = split(jnp.concatenate(half, axis=0).reshape(2 * HALF * 2 * TAB, 2 * cf).T)

    def inv_step(t, _):
        q = lax.rem(lax.div(me, GROUP) + t, nq)
        field = mm3(tt, (xyh[q], xyl[q]))
        total = jnp.zeros((fp, ch), F32)
        for c in range(2 * TAB):
            if c % TAB < HALF and c != TAB:
                total = total + ztab[q, c : c + 1, :] * field[c * fp : (c + 1) * fp]
        for i in range(GROUP):
            p = q * GROUP + i
            lng[p] = total[0:fpd, i * BLOCK : (i + 1) * BLOCK]

            @pl.when(p != me)
            def _():
                back_copy(p, me).start()

        return 0

    lax.fori_loop(0, nq, inv_step, 0)
    back[pl.ds(me, 1)] = lng[pl.ds(me, 1)]

    def wait_back(t, _):
        p = lax.rem(me + t, n)
        back_copy(p, p).wait_recv()
        return 0

    lax.fori_loop(1, n, wait_back, 0)
    for p in range(n):
        lt[p * fpd : (p + 1) * fpd, :] = back[p]
    total = out_ref[...] + lt[...].T
    normed = total * lax.rsqrt(jnp.mean(total * total, axis=1, keepdims=True) + EPS) * gain_ref[...]
    up = mm3(split(normed), split(wup_ref[...]))
    h = 0.5 * up
    out_ref[...] = total + mm3(split(h + h * jnp.tanh(h)), split(wdown_ref[...]))

    def wait_sent(t, _):
        p = lax.rem(me + t, n)
        feat_copy(p, me).wait_send()
        back_copy(p, me).wait_send()
        return 0

    lax.fori_loop(1, n, wait_sent, 0)

    def wait_spec_sent(t, _):
        spec_copy(lax.rem(mine + t, nj), mine).wait_send()
        return 0

    lax.fori_loop(1, nj, wait_spec_sent, 0)

    @pl.when(me + 1 < n)
    def _():
        halo_copy(0).wait_send()

    @pl.when(me > 0)
    def _():
        halo_copy(1).wait_send()


def local(
    sizes, features, positions, wavevectors, neighbour_slots, neighbour_count, pair_distance,
    w_self, w_neighbour, w_edge, w_message, spec_filter, norm_gain, w_up, w_down,
):
    nb, nw, ng = sizes
    n, nj = nb * nw * ng, nw * ng
    rows, width = features.shape
    kloc = spec_filter.shape[0]
    fpd = width // n
    fp = max(fpd, 16)
    cf = TAB * fp
    ch = GROUP * BLOCK
    nq = n // GROUP
    nxy = 2 * HALF * 2 * TAB
    mine = lax.dynamic_slice_in_dim(spec_filter, lax.axis_index("bead") * (nj * fpd), nj * fpd, 1)
    vectors = jnp.broadcast_to(wavevectors.astype(F32)[None], (nj, 3, kloc))
    spack = jnp.concatenate([mine.T.reshape(nj, fpd, kloc), vectors], axis=1)
    vmem = pl.BlockSpec(memory_space=pltpu.VMEM)
    dma = pltpu.SemaphoreType.DMA
    return pl.pallas_call(
        functools.partial(body, sizes),
        out_shape=jax.ShapeDtypeStruct((rows, width), F32),
        in_specs=[vmem] * 13,
        out_specs=vmem,
        scratch_shapes=[
            pltpu.VMEM((n, fpd + 6, BLOCK), F32),
            pltpu.VMEM((n, fpd + 6, BLOCK), F32),
            pltpu.VMEM((nj, fpd + 3, kloc), F32),
            pltpu.VMEM((2, rows, width), F32),
            pltpu.VMEM((nq, nxy, ch), BF16),
            pltpu.VMEM((nq, nxy, ch), BF16),
            pltpu.VMEM((nq, 2 * TAB, ch), F32),
            pltpu.VMEM((2 * TAB, ch), F32),
            pltpu.VMEM((2 * cf, ch), BF16),
            pltpu.VMEM((2 * cf, ch), BF16),
            pltpu.VMEM((nxy, 2 * cf), F32),
            pltpu.VMEM((n, fpd, BLOCK), F32),
            pltpu.VMEM((n, fpd, BLOCK), F32),
            pltpu.VMEM((width, rows), F32),
            pltpu.VMEM((width, 7 * BLOCK), BF16),
            pltpu.VMEM((width, rows), F32),
            pltpu.VMEM((width, rows), F32),
            pltpu.VMEM((4 * HALF * TAB, 3 * cf), F32),
            dma((n,)), dma((n,)), dma((nj,)), dma((nj,)), dma((2,)), dma((2,)), dma((n,)), dma((n,)),
        ],
        compiler_params=pltpu.CompilerParams(
            collective_id=0, has_side_effects=True, vmem_limit_bytes=60 * 1024 * 1024),
        cost_estimate=pl.CostEstimate(flops=10**10, bytes_accessed=10**7, transcendentals=10**7),
    )(
        features, positions, spack, neighbour_slots, neighbour_count[None], pair_distance,
        w_self, w_neighbour, w_edge, w_message, norm_gain[None], w_up, w_down,
    )


def solution(mesh):
    sizes = tuple(mesh.shape[a] for a in ("bead", "wave", "grp"))
    every = ("bead", "wave", "grp")
    placed = (
        P(every, None), P(None, every), P(None, ("wave", "grp")), P(None, every), P(every), P(None, every),
        P(), P(), P(), P(), P(("wave", "grp"), None), P(), P(), P(),
    )
    return jax.shard_map(
        functools.partial(local, sizes), mesh=mesh, in_specs=placed, out_specs=P(every, None), check_vma=False)
```

profile of v0, /device:TPU:0, one launch (start us, length us, event | category | flops | bytes accessed | tf_op | source)
XLA Modules:
  0.0 54.3 jit_solution(3963476491068422764)
XLA Ops:
  0.0 0.0 copy-start
  0.0 0.0 copy-start.1
  0.0 0.8 %copy-done.1 = s32[3,512]{1,0:T(4,128)S(1)} copy-done((s32[3,512]{1,0:T(4,128)S(1)}, s32[3,512]{1,0:T(4,128)}, u32[]{:S(2)}) %copy-start.1) | copy-done | bytes 6168
  0.8 0.4 copy-done
  1.3 0.1 copy.15
  1.4 0.8 %pad_maximum_fusion.spack_ref = f32[8,19,512]{2,1,0:T(8,128)} fusion(f32[8,3,512]{2,1,0:T(4,128)S(1)} %broadcast_in_dim.12, f32[8,16,512]{2,1,0:T(8,128)S(1)} %bitcast.5), kind=kLoop, calls=%fused_computation | loop fusion | flops 77824 | bytes 622592 | tf_op jit(solution)/shard_map/concatenate | solution.py:362
  2.2 50.4 %shard_map.136 = f32[128,512]{1,0:T(8,128)} custom-call(f32[128,512]{1,0:T(8,128)} %feat_ref.1, f32[3,128]{1,0:T(4,128)} %pos_ref.1, f32[8,19,512]{2,1,0:T(8,128)} %pad_maximum_fusion.spack_ref, s32[32,128]{1,0:T(8,128)} %slot_ref.1, s32[1,128]{1,0:T(1,128)} %bitcast.7, f32[32,128]{1,0:T(8,128)} %dist_ref.1, f32[512,512]{1,0:T(8,128)} %wself_ref.1, ...), custom_call_target="tpu_custom_call" | custom-call | flops 10000000000 | bytes 10000000 | tf_op jit(solution)/shard_map/pallas_call | solution.py:365
  52.6 1.7 %copy.17 = f32[128,512]{1,0:T(8,128)} copy(f32[128,512]{1,0:T(8,128)} %shard_map.136) | data formatting | bytes 524288
  (3 shorter events, 0.1 us)
Async XLA Ops:
  0.0 1.2 %copy-start = (f32[512,512]{1,0:T(8,128)S(1)}, f32[512,512]{1,0:T(8,128)}, u32[]{:S(2)}) copy-start(f32[512,512]{1,0:T(8,128)} %param.24) | copy-start | bytes 3145732
  0.0 0.8 %copy-start.1 = (s32[3,512]{1,0:T(4,128)S(1)}, s32[3,512]{1,0:T(4,128)}, u32[]{:S(2)}) copy-start(s32[3,512]{1,0:T(4,128)} %param.16) | copy-start | bytes 18436
where the time goes:
time: 54.5 us; the launch traced here: 54.3 us
  Pallas kernels  50.4 us (92%)
  local copies, waits for them, and re-layouts  3.07 us (6%)
  other arithmetic  0.79 us (1%)
    pallas_call x1, Pallas kernels, local(): pl.pallas_call(functools.partial(body, sizes), out_shape=jax.ShapeDtypeSt...  50.4 us
    unnamed x5, local copies, waits for them, and re-layouts  2.89 us

commit v1 on v0

--- a/solution.py
+++ b/solution.py
@@ -35,12 +35,12 @@
 
 def body(
     sizes,
-    feat_ref, pos_ref, spack_ref, slot_ref, count_ref, dist_ref,
-    wself_ref, wneigh_ref, wedge_ref, wmsg_ref, gain_ref, wup_ref, wdown_ref,
+    feat_ref, pos_ref, wave_ref, slot_ref, count_ref, dist_ref, wedge_ref, gain_ref,
+    spec_hbm, wself_hbm, wneigh_hbm, wmsg_hbm, wup_hbm, wdown_hbm,
     out_ref,
-    pack, fall, spall, halo, xyh, xyl, ztab, ytab, ah, al, tacc, lng, back, lt,
-    wt, selft, acc, gacc,
-    fs, fr, ss, sr, hs, hr, bs, br,
+    pack, fall, spack, spall, tall, wall, halo, xyh, xyl, ztab, ytab, ah, al, tacc, lng, back, lt,
+    wt, selft, acc, gacc, spec, weights,
+    fs, fr, ss, sr, hs, hr, bs, br, t1s, t1r, t2s, t2r, w1s, w1r, w2s, w2r, ls,
 ):
     nb, nw, ng = sizes
     n, nj = nb * nw * ng, nw * ng
@@ -50,7 +50,9 @@
     cf = TAB * fp
     ch = GROUP * BLOCK
     nq = n // GROUP
-    kloc = spack_ref.shape[2]
+    kloc = spec_hbm.shape[0]
+    cols = nj * fpd
+    nr = nb * ng
     ib, iw, ig = lax.axis_index("bead"), lax.axis_index("wave"), lax.axis_index("grp")
     mine = iw * ng + ig
     me = ib * nj + mine
@@ -58,6 +60,14 @@
     def coords(p):
         return (lax.div(p, nj), lax.rem(lax.div(p, ng), nw), lax.rem(p, ng))
 
+    at = ib * cols
+    source = spec_hbm if cols % 128 else spec_hbm.at[:, pl.ds(pl.multiple_of(at, 128), cols)]
+    fetch = [pltpu.make_async_copy(source, spec, ls.at[0])]
+    for i, w in enumerate((wself_hbm, wneigh_hbm, wmsg_hbm, wup_hbm, wdown_hbm)):
+        fetch.append(pltpu.make_async_copy(w, weights.at[i], ls.at[i + 1]))
+    for copy in fetch:
+        copy.start()
+
     barrier = pltpu.get_barrier_semaphore()
 
     def greet(t, _):
@@ -68,11 +78,30 @@
 
     ft = feat_ref[...].T
     angle = TWO_PI * pos_ref[...]
-    trig = jnp.concatenate([jnp.cos(angle), jnp.sin(angle)], axis=0)
+    trig = jnp.concatenate([jnp.cos(angle), jnp.sin(angle), jnp.zeros((2, rows), F32)], axis=0)
+    tall[ib, ig, iw] = trig
+    wall[ig, iw] = wave_ref[...]
     for p in range(n):
-        pack[p, 0:fpd, :] = ft[p * fpd : (p + 1) * fpd]
-        pack[p, fpd : fpd + 6, :] = trig
+        pack[p] = ft[p * fpd : (p + 1) * fpd]
     pl.semaphore_wait(barrier, n - 1)
+
+    def along_copies(w, slot):
+        return [pltpu.make_async_remote_copy(
+            src_ref=buf.at[ig, iw] if buf is wall else buf.at[ib, ig, iw],
+            dst_ref=buf.at[ig, slot] if buf is wall else buf.at[ib, ig, slot],
+            send_sem=send.at[w], recv_sem=recv.at[slot],
+            device_id=(ib, w, ig), device_id_type=MESH) for buf, send, recv in ((tall, t1s, t1r), (wall, w1s, w1r))]
+
+    def plane_copy(r, slot):
+        b, g = lax.div(slot, ng), lax.rem(slot, ng)
+        return pltpu.make_async_remote_copy(
+            src_ref=tall.at[ib, ig], dst_ref=tall.at[b, g], send_sem=t2s.at[r], recv_sem=t2r.at[slot],
+            device_id=(lax.div(r, ng), iw, lax.rem(r, ng)), device_id_type=MESH)
+
+    def core_copy(g, slot):
+        return pltpu.make_async_remote_copy(
+            src_ref=wall.at[ig], dst_ref=wall.at[slot], send_sem=w2s.at[g], recv_sem=w2r.at[slot],
+            device_id=(ib, iw, g), device_id_type=MESH)
 
     def feat_copy(p, slot):
         return pltpu.make_async_remote_copy(
@@ -81,7 +110,7 @@
 
     def spec_copy(j, slot):
         return pltpu.make_async_remote_copy(
-            src_ref=spack_ref.at[j], dst_ref=spall.at[slot], send_sem=ss.at[j], recv_sem=sr.at[slot],
+            src_ref=spack.at[j], dst_ref=spall.at[slot], send_sem=ss.at[j], recv_sem=sr.at[slot],
             device_id=coords(ib * nj + j), device_id_type=MESH)
 
     def halo_copy(side):
@@ -95,27 +124,49 @@
             src_ref=lng.at[p], dst_ref=back.at[slot], send_sem=bs.at[p], recv_sem=br.at[slot],
             device_id=coords(p), device_id_type=MESH)
 
-    @pl.when(me + 1 < n)
-    def _():
-        halo_copy(0).start()
-
-    @pl.when(me > 0)
-    def _():
-        halo_copy(1).start()
-
-    def send_feat(t, _):
-        feat_copy(lax.rem(me + t, n), me).start()
-        return 0
-
-    lax.fori_loop(1, n, send_feat, 0)
+    for k in range(1, nw):
+        for copy in along_copies(lax.rem(iw + k, nw), iw):
+            copy.start()
+    here = ib * ng + ig
+    far = sorted(range(nw), key=lambda k: -min(k, nw - k))
+    for k in far:
+        w = lax.rem(iw + k, nw)
+
+        def send_feat(t, _):
+            r = lax.rem(here + t, nr)
+            feat_copy((lax.div(r, ng) * nw + w) * ng + lax.rem(r, ng), me).start()
+            return 0
+
+        lax.fori_loop(0 if k else 1, nr, send_feat, 0)
+
+    fetch[0].wait()
+    st = spec[...].T
+    for j in range(nj):
+        spack[j] = st[j * fpd : (j + 1) * fpd]
+    for k in range(1, nw):
+        for copy in along_copies(iw, lax.rem(iw + k, nw)):
+            copy.wait_recv()
+
+    def send_plane(t, _):
+        plane_copy(lax.rem(here + t, nr), here).start()
+        return 0
+
+    lax.fori_loop(1, nr, send_plane, 0)
+    for k in range(1, ng):
+        core_copy(lax.rem(ig + k, ng), ig).start()
 
     def send_spec(t, _):
-        spec_copy(lax.rem(mine + t, nj), mine).start()
-        return 0
-
-    lax.fori_loop(1, nj, send_spec, 0)
+        j = lax.rem(mine + nj // 2 + t, nj)
+
+        @pl.when(j != mine)
+        def _():
+            spec_copy(j, mine).start()
+
+        return 0
+
+    lax.fori_loop(0, nj, send_spec, 0)
     fall[pl.ds(me, 1)] = pack[pl.ds(me, 1)]
-    spall[pl.ds(mine, 1)] = spack_ref[pl.ds(mine, 1)]
+    spall[pl.ds(mine, 1)] = spack[pl.ds(mine, 1)]
 
     @pl.when(me == 0)
     def _():
@@ -125,9 +176,11 @@
     def _():
         halo[1] = jnp.zeros((rows, width), F32)
 
+    fetch[1].wait()
     own = split(feat_ref[...])
-    selft[...] = 0.5 * mm3(own, split(wself_ref[...])).T
-    wn = split(wneigh_ref[...])
+    selft[...] = 0.5 * mm3(own, split(weights[0])).T
+    fetch[2].wait()
+    wn = split(weights[1])
     span = 3 * BLOCK
 
     def put_window(at, part):
@@ -141,79 +194,27 @@
     wt[:, 2 * span : 2 * span + BLOCK] = jnp.concatenate(
         [eh, eh, el, jnp.zeros((width, BLOCK - 3 * radial), BF16)], axis=1)
 
-    @pl.when(me > 0)
-    def _():
-        halo_copy(0).wait_recv()
-
-    @pl.when(me + 1 < n)
-    def _():
-        halo_copy(1).wait_recv()
-
-    put_window(0, split(halo[0]))
-    put_window(2, split(halo[1]))
-
-    acc[...] = jnp.zeros((width, rows), F32)
-    spacing = REACH / (radial - 1)
-    centers = lax.broadcasted_iota(jnp.int32, (radial, rows), 0).astype(F32) * spacing
-    row_id = lax.broadcasted_iota(jnp.int32, (span, rows), 0)
-    slots = slot_ref.shape[0]
-    count = count_ref[...]
-
-    def short_step(t, _):
-        parts = []
-        for u in range(SLOTS):
-            s = t * SLOTS + u
-            one = jnp.where(row_id == slot_ref[pl.ds(s, 1), :], 1.0, 0.0).astype(BF16)
-            bh, bl = split(jnp.exp(-jnp.square((dist_ref[pl.ds(s, 1), :] - centers) / spacing)))
-            parts.append(jnp.concatenate(
-                [one, one, bh, bl, bh, jnp.zeros((BLOCK - 3 * radial, rows), BF16)], axis=0))
-        pre = dot(wt[...], jnp.concatenate(parts, axis=1))
-        total = acc[...]
-        for u in range(SLOTS):
-            h = pre[:, u * rows : (u + 1) * rows] + selft[...]
-            live = count > t * SLOTS + u
-            total = total + jnp.where(live, h + h * jnp.tanh(h), 0.0)
-        acc[...] = total
-        return 0
-
-    lax.fori_loop(0, slots // SLOTS, short_step, 0)
-    short = mm3(split((acc[...] * (1.0 / slots)).T), split(wmsg_ref[...]))
-    out_ref[...] = feat_ref[...] + short
-
-    def wait_spec(t, _):
-        j = lax.rem(mine + t, nj)
-        spec_copy(j, j).wait_recv()
-        return 0
-
-    lax.fori_loop(1, nj, wait_spec, 0)
-    nvec = 4 * HALF * TAB
-    gacc[...] = jnp.zeros(gacc.shape, F32)
-
-    def spec_step(j, _):
-        sp = spall[j, 0:fpd, :]
-        if fp > fpd:
-            sp = jnp.concatenate([sp, jnp.zeros((fp - fpd, kloc), F32)], axis=0)
-        kx, ky, kz = (spall[j, fpd + i : fpd + i + 1, :] for i in range(3))
-        flip = jnp.where(kx < 0, -1.0, 1.0)
-        ky, kz = ky * flip, kz * flip
-        kind = jnp.where(ky < 0, 2.0, 0.0) + jnp.where(kz < 0, 1.0, 0.0)
-        at = kind * (HALF * TAB) + jnp.abs(kx) * TAB + jnp.abs(ky)
-        vec_id = lax.broadcasted_iota(jnp.int32, (nvec, kloc), 0).astype(F32)
-        pick = jnp.where(vec_id == at, 1.0, 0.0).astype(BF16)
-        c = jnp.abs(kz)
-        vals = jnp.concatenate([jnp.where(c == i, sp, 0.0) for i in range(TAB)], axis=0)
-        hits = jnp.concatenate(
-            [jnp.broadcast_to(jnp.where(c == i, 1.0, 0.0), (fp, kloc)) for i in range(TAB)], axis=0)
-        vh, vl = split(vals)
-        gacc[...] += dot(pick, jnp.concatenate([vh, vl, hits.astype(BF16)], axis=0), 1, 1)
-        return 0
-
-    lax.fori_loop(0, nj, spec_step, 0)
+    for i in range(3, 6):
+        fetch[i].wait()
 
     tacc[...] = jnp.zeros(tacc.shape, F32)
 
+    def wait_plane(t, _):
+        r = lax.rem(here + t, nr)
+        plane_copy(r, r).wait_recv()
+        return 0
+
+    lax.fori_loop(1, nr, wait_plane, 0)
+    for k in range(1, ng):
+        core_copy(ig, lax.rem(ig + k, ng)).wait_recv()
+    per = nq // nb
+    first = lax.div(mine, GROUP)
+
+    def chunk(t):
+        return lax.rem(ib + t, nb) * per + lax.rem(first + lax.div(t, nb), per)
+
     def fwd_step(t, _):
-        q = lax.rem(lax.div(me, GROUP) + t, nq)
+        q = chunk(t)
         for i in range(GROUP):
             p = q * GROUP + i
 
@@ -222,11 +223,12 @@
                 feat_copy(p, p).wait_recv()
 
         blocks = [fall[q * GROUP + i] for i in range(GROUP)]
-        f = jnp.concatenate([b[0:fpd] for b in blocks], axis=1)
+        f = jnp.concatenate(blocks, axis=1)
         if fp > fpd:
             f = jnp.concatenate([f, jnp.zeros((fp - fpd, ch), F32)], axis=0)
-        c1 = jnp.concatenate([b[fpd : fpd + 3] for b in blocks], axis=1)
-        s1 = jnp.concatenate([b[fpd + 3 : fpd + 6] for b in blocks], axis=1)
+        places = [(lax.div(p, nj), lax.rem(p, ng), lax.rem(lax.div(p, ng), nw)) for p in [q * GROUP + i for i in range(GROUP)]]
+        trigs = jnp.concatenate([tall[b, g, w] for b, g, w in places], axis=1)
+        c1, s1 = trigs[0:3], trigs[3:6]
         cs, sn = [jnp.ones_like(c1), c1], [jnp.zeros_like(c1), s1]
         for a in range(2, HALF):
             cs.append(cs[-1] * c1 - sn[-1] * s1)
@@ -255,6 +257,45 @@
 
     lax.fori_loop(0, nq, fwd_step, 0)
 
+    @pl.when(me + 1 < n)
+    def _():
+        halo_copy(0).start()
+
+    @pl.when(me > 0)
+    def _():
+        halo_copy(1).start()
+
+    def wait_spec(t, _):
+        j = lax.rem(mine + t, nj)
+        spec_copy(j, j).wait_recv()
+        return 0
+
+    lax.fori_loop(1, nj, wait_spec, 0)
+    nvec = 4 * HALF * TAB
+    gacc[...] = jnp.zeros(gacc.shape, F32)
+
+    def spec_step(j, _):
+        sp = spall[j]
+        if fp > fpd:
+            sp = jnp.concatenate([sp, jnp.zeros((fp - fpd, kloc), F32)], axis=0)
+        vec = wall[lax.rem(j, ng), lax.div(j, ng)].astype(F32)
+        kx, ky, kz = (vec[i : i + 1] for i in range(3))
+        flip = jnp.where(kx < 0, -1.0, 1.0)
+        ky, kz = ky * flip, kz * flip
+        kind = jnp.where(ky < 0, 2.0, 0.0) + jnp.where(kz < 0, 1.0, 0.0)
+        at = kind * (HALF * TAB) + jnp.abs(kx) * TAB + jnp.abs(ky)
+        vec_id = lax.broadcasted_iota(jnp.int32, (nvec, kloc), 0).astype(F32)
+        pick = jnp.where(vec_id == at, 1.0, 0.0).astype(BF16)
+        c = jnp.abs(kz)
+        vals = jnp.concatenate([jnp.where(c == i, sp, 0.0) for i in range(TAB)], axis=0)
+        hits = jnp.concatenate(
+            [jnp.broadcast_to(jnp.where(c == i, 1.0, 0.0), (fp, kloc)) for i in range(TAB)], axis=0)
+        vh, vl = split(vals)
+        gacc[...] += dot(pick, jnp.concatenate([vh, vl, hits.astype(BF16)], axis=0), 1, 1)
+        return 0
+
+    lax.fori_loop(0, nj, spec_step, 0)
+
     nt = HALF * TAB
     t3 = tacc[...].reshape(2 * HALF, 2 * TAB, 2 * cf)
 
@@ -287,7 +328,7 @@
     tt = split(jnp.concatenate(half, axis=0).reshape(2 * HALF * 2 * TAB, 2 * cf).T)
 
     def inv_step(t, _):
-        q = lax.rem(lax.div(me, GROUP) + t, nq)
+        q = chunk(nq - 1 - t)
         field = mm3(tt, (xyh[q], xyl[q]))
         total = jnp.zeros((fp, ch), F32)
         for c in range(2 * TAB):
@@ -306,6 +347,46 @@
     lax.fori_loop(0, nq, inv_step, 0)
     back[pl.ds(me, 1)] = lng[pl.ds(me, 1)]
 
+    @pl.when(me > 0)
+    def _():
+        halo_copy(0).wait_recv()
+
+    @pl.when(me + 1 < n)
+    def _():
+        halo_copy(1).wait_recv()
+
+    put_window(0, split(halo[0]))
+    put_window(2, split(halo[1]))
+
+    acc[...] = jnp.zeros((width, rows), F32)
+    spacing = REACH / (radial - 1)
+    centers = lax.broadcasted_iota(jnp.int32, (radial, rows), 0).astype(F32) * spacing
+    row_id = lax.broadcasted_iota(jnp.int32, (span, rows), 0)
+    slots = slot_ref.shape[0]
+    count = count_ref[...]
+
+    def short_step(t, _):
+        parts = []
+        for u in range(SLOTS):
+            s = t * SLOTS + u
+            one = jnp.where(row_id == slot_ref[pl.ds(s, 1), :], 1.0, 0.0).astype(BF16)
+            bh, bl = split(jnp.exp(-jnp.square((dist_ref[pl.ds(s, 1), :] - centers) / spacing)))
+            parts.append(jnp.concatenate(
+                [one, one, bh, bl, bh, jnp.zeros((BLOCK - 3 * radial, rows), BF16)], axis=0))
+        pre = dot(wt[...], jnp.concatenate(parts, axis=1))
+        total = acc[...]
+        for u in range(SLOTS):
+            h = pre[:, u * rows : (u + 1) * rows] + selft[...]
+            live = count > t * SLOTS + u
+            total = total + jnp.where(live, h + h * jnp.tanh(h), 0.0)
+        acc[...] = total
+        return 0
+
+    lax.fori_loop(0, slots // SLOTS, short_step, 0)
+    short = mm3(split((acc[...] * (1.0 / slots)).T), split(weights[2]))
+    out_ref[...] = feat_ref[...] + short
+
+
     def wait_back(t, _):
         p = lax.rem(me + t, n)
         back_copy(p, p).wait_recv()
@@ -316,9 +397,9 @@
         lt[p * fpd : (p + 1) * fpd, :] = back[p]
     total = out_ref[...] + lt[...].T
     normed = total * lax.rsqrt(jnp.mean(total * total, axis=1, keepdims=True) + EPS) * gain_ref[...]
-    up = mm3(split(normed), split(wup_ref[...]))
+    up = mm3(split(normed), split(weights[3]))
     h = 0.5 * up
-    out_ref[...] = total + mm3(split(h + h * jnp.tanh(h)), split(wdown_ref[...]))
+    out_ref[...] = total + mm3(split(h + h * jnp.tanh(h)), split(weights[4]))
 
     def wait_sent(t, _):
         p = lax.rem(me + t, n)
@@ -327,6 +408,18 @@
         return 0
 
     lax.fori_loop(1, n, wait_sent, 0)
+
+    for k in range(1, nw):
+        for copy in along_copies(lax.rem(iw + k, nw), iw):
+            copy.wait_send()
+
+    def wait_plane_sent(t, _):
+        plane_copy(lax.rem(here + t, nr), here).wait_send()
+        return 0
+
+    lax.fori_loop(1, nr, wait_plane_sent, 0)
+    for k in range(1, ng):
+        core_copy(lax.rem(ig + k, ng), ig).wait_send()
 
     def wait_spec_sent(t, _):
         spec_copy(lax.rem(mine + t, nj), mine).wait_send()
@@ -357,20 +450,23 @@
     ch = GROUP * BLOCK
     nq = n // GROUP
     nxy = 2 * HALF * 2 * TAB
-    mine = lax.dynamic_slice_in_dim(spec_filter, lax.axis_index("bead") * (nj * fpd), nj * fpd, 1)
-    vectors = jnp.broadcast_to(wavevectors.astype(F32)[None], (nj, 3, kloc))
-    spack = jnp.concatenate([mine.T.reshape(nj, fpd, kloc), vectors], axis=1)
+    cols = nj * fpd
+    if cols % 128:
+        spec_filter = lax.dynamic_slice_in_dim(spec_filter, lax.axis_index("bead") * cols, cols, 1)
     vmem = pl.BlockSpec(memory_space=pltpu.VMEM)
     dma = pltpu.SemaphoreType.DMA
     return pl.pallas_call(
         functools.partial(body, sizes),
         out_shape=jax.ShapeDtypeStruct((rows, width), F32),
-        in_specs=[vmem] * 13,
+        in_specs=[vmem] * 8 + [pl.BlockSpec(memory_space=pl.ANY)] * 6,
         out_specs=vmem,
         scratch_shapes=[
-            pltpu.VMEM((n, fpd + 6, BLOCK), F32),
-            pltpu.VMEM((n, fpd + 6, BLOCK), F32),
-            pltpu.VMEM((nj, fpd + 3, kloc), F32),
+            pltpu.VMEM((n, fpd, BLOCK), F32),
+            pltpu.VMEM((n, fpd, BLOCK), F32),
+            pltpu.VMEM((nj, fpd, kloc), F32),
+            pltpu.VMEM((nj, fpd, kloc), F32),
+            pltpu.VMEM((nb, ng, nw, 8, BLOCK), F32),
+            pltpu.VMEM((ng, nw, 3, kloc), jnp.int32),
             pltpu.VMEM((2, rows, width), F32),
             pltpu.VMEM((nq, nxy, ch), BF16),
             pltpu.VMEM((nq, nxy, ch), BF16),
@@ -386,14 +482,17 @@
             pltpu.VMEM((width, rows), F32),
             pltpu.VMEM((width, rows), F32),
             pltpu.VMEM((4 * HALF * TAB, 3 * cf), F32),
+            pltpu.VMEM((kloc, cols), F32),
+            pltpu.VMEM((5, width, width), F32),
             dma((n,)), dma((n,)), dma((nj,)), dma((nj,)), dma((2,)), dma((2,)), dma((n,)), dma((n,)),
+            dma((nw,)), dma((nw,)), dma((nb * ng,)), dma((nb * ng,)), dma((nw,)), dma((nw,)), dma((ng,)), dma((ng,)), dma((6,)),
         ],
         compiler_params=pltpu.CompilerParams(
             collective_id=0, has_side_effects=True, vmem_limit_bytes=60 * 1024 * 1024),
         cost_estimate=pl.CostEstimate(flops=10**10, bytes_accessed=10**7, transcendentals=10**7),
     )(
-        features, positions, spack, neighbour_slots, neighbour_count[None], pair_distance,
-        w_self, w_neighbour, w_edge, w_message, norm_gain[None], w_up, w_down,
+        features, positions, wavevectors, neighbour_slots, neighbour_count[None], pair_distance,
+        w_edge, norm_gain[None], spec_filter, w_self, w_neighbour, w_message, w_up, w_down,
     )
 
 

time: 54.5 us -> 44.9 us (0.82)
  the two profiles are of different devices: /device:TPU:0 before, /device:TPU:11 now
where the time goes in v1:
time: 44.9 us; the launch traced here: 44.7 us
  Pallas kernels  43 us (96%)
  local copies, waits for them, and re-layouts  1.67 us (4%)
    pallas_call x1, Pallas kernels, local(): pl.pallas_call(functools.partial(body, sizes), out_shape=jax.ShapeDtypeSt...  43 us
    unnamed x1, local copies, waits for them, and re-layouts  1.67 us

profile of v1, /device:TPU:11, one launch (start us, length us, event | category | flops | bytes accessed | tf_op | source)
XLA Modules:
  0.0 44.7 jit_solution(14187994159524098985)
XLA Ops:
  0.0 43.0 %shard_map.136 = f32[128,512]{1,0:T(8,128)} custom-call(f32[128,512]{1,0:T(8,128)} %feat_ref.1, f32[3,128]{1,0:T(4,128)} %pos_ref.1, s32[3,512]{1,0:T(4,128)} %wave_ref.1, s32[32,128]{1,0:T(8,128)} %slot_ref.1, s32[1,128]{1,0:T(1,128)} %bitcast.3, f32[32,128]{1,0:T(8,128)} %dist_ref.1, f32[16,512]{1,0:T(8,128)} %wedge_ref.1, f32[1,512]{1,0:T(1,128)} %bitcast.2, ...), custom_call_target="tpu_custom_call" | custom-call | flops 10000000000 | bytes 10000000 | tf_op jit(solution)/shard_map/pallas_call | solution.py:458
  43.0 1.7 %copy.16 = f32[128,512]{1,0:T(8,128)} copy(f32[128,512]{1,0:T(8,128)} %shard_map.136) | data formatting | bytes 524288

commit v2 on v1

--- a/solution.py
+++ b/solution.py
@@ -39,7 +39,7 @@
     spec_hbm, wself_hbm, wneigh_hbm, wmsg_hbm, wup_hbm, wdown_hbm,
     out_ref,
     pack, fall, spack, spall, tall, wall, halo, xyh, xyl, ztab, ytab, ah, al, tacc, lng, back, lt,
-    wt, selft, acc, gacc, spec, weights,
+    wt, selft, acc, gacc, spec, weights, wide,
     fs, fr, ss, sr, hs, hr, bs, br, t1s, t1r, t2s, t2r, w1s, w1r, w2s, w2r, ls,
 ):
     nb, nw, ng = sizes
@@ -184,18 +184,17 @@
     span = 3 * BLOCK
 
     def put_window(at, part):
-        hi, lo = split(0.5 * mm3(part, wn).T)
-        wt[:, at * BLOCK : (at + 1) * BLOCK] = hi
-        wt[:, span + at * BLOCK : span + (at + 1) * BLOCK] = lo
+        wt[:, at * BLOCK : (at + 1) * BLOCK] = (0.5 * mm3(part, wn)).T.astype(BF16)
 
     put_window(1, own)
     radial = wedge_ref.shape[0]
     eh, el = split(0.5 * wedge_ref[...].T)
-    wt[:, 2 * span : 2 * span + BLOCK] = jnp.concatenate(
+    wt[:, span : span + BLOCK] = jnp.concatenate(
         [eh, eh, el, jnp.zeros((width, BLOCK - 3 * radial), BF16)], axis=1)
 
-    for i in range(3, 6):
-        fetch[i].wait()
+    for i in range(3):
+        fetch[i + 3].wait()
+        wide[i, 0], wide[i, 1] = split(weights[i + 2])
 
     tacc[...] = jnp.zeros(tacc.shape, F32)
 
@@ -215,6 +214,15 @@
 
     def fwd_step(t, _):
         q = chunk(t)
+
+        @pl.when((t == nq // 2) & (me + 1 < n))
+        def _():
+            halo_copy(0).start()
+
+        @pl.when((t == nq // 2) & (me > 0))
+        def _():
+            halo_copy(1).start()
+
         for i in range(GROUP):
             p = q * GROUP + i
 
@@ -257,14 +265,6 @@
 
     lax.fori_loop(0, nq, fwd_step, 0)
 
-    @pl.when(me + 1 < n)
-    def _():
-        halo_copy(0).start()
-
-    @pl.when(me > 0)
-    def _():
-        halo_copy(1).start()
-
     def wait_spec(t, _):
         j = lax.rem(mine + t, nj)
         spec_copy(j, j).wait_recv()
@@ -372,7 +372,7 @@
             one = jnp.where(row_id == slot_ref[pl.ds(s, 1), :], 1.0, 0.0).astype(BF16)
             bh, bl = split(jnp.exp(-jnp.square((dist_ref[pl.ds(s, 1), :] - centers) / spacing)))
             parts.append(jnp.concatenate(
-                [one, one, bh, bl, bh, jnp.zeros((BLOCK - 3 * radial, rows), BF16)], axis=0))
+                [one, bh, bl, bh, jnp.zeros((BLOCK - 3 * radial, rows), BF16)], axis=0))
         pre = dot(wt[...], jnp.concatenate(parts, axis=1))
         total = acc[...]
         for u in range(SLOTS):
@@ -383,7 +383,7 @@
         return 0
 
     lax.fori_loop(0, slots // SLOTS, short_step, 0)
-    short = mm3(split((acc[...] * (1.0 / slots)).T), split(weights[2]))
+    short = mm3(split((acc[...] * (1.0 / slots)).T), (wide[0, 0], wide[0, 1]))
     out_ref[...] = feat_ref[...] + short
 
 
@@ -397,9 +397,9 @@
         lt[p * fpd : (p + 1) * fpd, :] = back[p]
     total = out_ref[...] + lt[...].T
     normed = total * lax.rsqrt(jnp.mean(total * total, axis=1, keepdims=True) + EPS) * gain_ref[...]
-    up = mm3(split(normed), split(weights[3]))
+    up = mm3(split(normed), (wide[1, 0], wide[1, 1]))
     h = 0.5 * up
-    out_ref[...] = total + mm3(split(h + h * jnp.tanh(h)), split(weights[4]))
+    out_ref[...] = total + mm3(split(h + h * jnp.tanh(h)), (wide[2, 0], wide[2, 1]))
 
     def wait_sent(t, _):
         p = lax.rem(me + t, n)
@@ -478,12 +478,13 @@
             pltpu.VMEM((n, fpd, BLOCK), F32),
             pltpu.VMEM((n, fpd, BLOCK), F32),
             pltpu.VMEM((width, rows), F32),
-            pltpu.VMEM((width, 7 * BLOCK), BF16),
+            pltpu.VMEM((width, 4 * BLOCK), BF16),
             pltpu.VMEM((width, rows), F32),
             pltpu.VMEM((width, rows), F32),
             pltpu.VMEM((4 * HALF * TAB, 3 * cf), F32),
             pltpu.VMEM((kloc, cols), F32),
             pltpu.VMEM((5, width, width), F32),
+            pltpu.VMEM((3, 2, width, width), BF16),
             dma((n,)), dma((n,)), dma((nj,)), dma((nj,)), dma((2,)), dma((2,)), dma((n,)), dma((n,)),
             dma((nw,)), dma((nw,)), dma((nb * ng,)), dma((nb * ng,)), dma((nw,)), dma((nw,)), dma((ng,)), dma((ng,)), dma((6,)),
         ],

time: 44.9 us -> 40.6 us (0.904)
  the two profiles are of different devices: /device:TPU:11 before, /device:TPU:0 now
where the time goes in v2:
time: 40.6 us; the launch traced here: 40.5 us
  Pallas kernels  38.8 us (96%)
  local copies, waits for them, and re-layouts  1.67 us (4%)
    pallas_call x1, Pallas kernels, local(): pl.pallas_call(functools.partial(body, sizes), out_shape=jax.ShapeDtypeSt...  38.8 us
    unnamed x1, local copies, waits for them, and re-layouts  1.67 us

profile of v2, /device:TPU:0, one launch (start us, length us, event | category | flops | bytes accessed | tf_op | source)
XLA Modules:
  0.0 40.5 jit_solution(8299619763292466733)
XLA Ops:
  0.0 38.8 %shard_map.136 = f32[128,512]{1,0:T(8,128)} custom-call(f32[128,512]{1,0:T(8,128)} %feat_ref.1, f32[3,128]{1,0:T(4,128)} %pos_ref.1, s32[3,512]{1,0:T(4,128)} %wave_ref.1, s32[32,128]{1,0:T(8,128)} %slot_ref.1, s32[1,128]{1,0:T(1,128)} %bitcast.3, f32[32,128]{1,0:T(8,128)} %dist_ref.1, f32[16,512]{1,0:T(8,128)} %wedge_ref.1, f32[1,512]{1,0:T(1,128)} %bitcast.2, ...), custom_call_target="tpu_custom_call" | custom-call | flops 10000000000 | bytes 10000000 | tf_op jit(solution)/shard_map/pallas_call | solution.py:458
  38.8 1.7 %copy.16 = f32[128,512]{1,0:T(8,128)} copy(f32[128,512]{1,0:T(8,128)} %shard_map.136) | data formatting | bytes 524288

commit v3 on v2

--- a/solution.py
+++ b/solution.py
@@ -184,12 +184,14 @@
     span = 3 * BLOCK
 
     def put_window(at, part):
-        wt[:, at * BLOCK : (at + 1) * BLOCK] = (0.5 * mm3(part, wn)).T.astype(BF16)
+        hi, lo = split(0.5 * mm3(part, wn).T)
+        wt[:, at * BLOCK : (at + 1) * BLOCK] = hi
+        wt[:, span + at * BLOCK : span + (at + 1) * BLOCK] = lo
 
     put_window(1, own)
     radial = wedge_ref.shape[0]
     eh, el = split(0.5 * wedge_ref[...].T)
-    wt[:, span : span + BLOCK] = jnp.concatenate(
+    wt[:, 2 * span : 2 * span + BLOCK] = jnp.concatenate(
         [eh, eh, el, jnp.zeros((width, BLOCK - 3 * radial), BF16)], axis=1)
 
     for i in range(3):
@@ -372,7 +374,7 @@
             one = jnp.where(row_id == slot_ref[pl.ds(s, 1), :], 1.0, 0.0).astype(BF16)
             bh, bl = split(jnp.exp(-jnp.square((dist_ref[pl.ds(s, 1), :] - centers) / spacing)))
             parts.append(jnp.concatenate(
-                [one, bh, bl, bh, jnp.zeros((BLOCK - 3 * radial, rows), BF16)], axis=0))
+                [one, one, bh, bl, bh, jnp.zeros((BLOCK - 3 * radial, rows), BF16)], axis=0))
         pre = dot(wt[...], jnp.concatenate(parts, axis=1))
         total = acc[...]
         for u in range(SLOTS):
@@ -478,7 +480,7 @@
             pltpu.VMEM((n, fpd, BLOCK), F32),
             pltpu.VMEM((n, fpd, BLOCK), F32),
             pltpu.VMEM((width, rows), F32),
-            pltpu.VMEM((width, 4 * BLOCK), BF16),
+            pltpu.VMEM((width, 7 * BLOCK), BF16),
             pltpu.VMEM((width, rows), F32),
             pltpu.VMEM((width, rows), F32),
             pltpu.VMEM((4 * HALF * TAB, 3 * cf), F32),

time: 40.6 us -> 43.2 us (1.064)
  Pallas kernels: 38.8 us -> 41.4 us
    pallas_call x1, Pallas kernels: 38.8 us -> 41.4 us  [local(): pl.pallas_call(functools.partial(body, sizes), out_shape=jax.ShapeDtypeSt...]
where the time goes in v3:
time: 43.2 us; the launch traced here: 43.1 us
  Pallas kernels  41.4 us (96%)
  local copies, waits for them, and re-layouts  1.67 us (4%)
    pallas_call x1, Pallas kernels, local(): pl.pallas_call(functools.partial(body, sizes), out_shape=jax.ShapeDtypeSt...  41.4 us
    unnamed x1, local copies, waits for them, and re-layouts  1.67 us

profile of v3, /device:TPU:0, one launch (start us, length us, event | category | flops | bytes accessed | tf_op | source)
XLA Modules:
  0.0 43.1 jit_solution(1444551844371946249)
XLA Ops:
  0.0 41.4 %shard_map.136 = f32[128,512]{1,0:T(8,128)} custom-call(f32[128,512]{1,0:T(8,128)} %feat_ref.1, f32[3,128]{1,0:T(4,128)} %pos_ref.1, s32[3,512]{1,0:T(4,128)} %wave_ref.1, s32[32,128]{1,0:T(8,128)} %slot_ref.1, s32[1,128]{1,0:T(1,128)} %bitcast.3, f32[32,128]{1,0:T(8,128)} %dist_ref.1, f32[16,512]{1,0:T(8,128)} %wedge_ref.1, f32[1,512]{1,0:T(1,128)} %bitcast.2, ...), custom_call_target="tpu_custom_call" | custom-call | flops 10000000000 | bytes 10000000 | tf_op jit(solution)/shard_map/pallas_call | solution.py:460
  41.4 1.7 %copy.16 = f32[128,512]{1,0:T(8,128)} copy(f32[128,512]{1,0:T(8,128)} %shard_map.136) | data formatting | bytes 524288
